TPU v7x, 32 devices: a whole 2x2x4 slice. The times are simulated.
32 devices in a mesh: ens: 2 (over y), gx: 4 (over z), ta: 2 (over x), col: 2 (over core).
Axes of the slice: x: 2, y: 2, z: 4, core: 2. Of those that a mesh axis runs over, the one named last changes fastest.
Arguments:
- frames: bfloat16 [40, 4, 128, 128, 128], P('ens', 'ta', 'gx', 'col'), parts along dimension 0, may hold values from -6 to 6
- counts: int32 [8], P('ens'), parts along dimension 0, may hold values from 1 to 3
- spectral_weight: bfloat16 [2, 40, 20, 65536], P(None, 'ens', 'col', 'gx'), parts along dimension 1, may hold values from -6 to 6
- point_weight: bfloat16 [40, 20], P('ens'), parts along dimension 0, may hold values from -1.25 to 1.25
- point_bias: float32 [40], P('ens'), parts along dimension 0, may hold values from -3 to 3
Outputs:
- layer_out: bfloat16 [40, 4, 128, 128, 128], P('ens', 'ta', 'gx', 'col'), parts along dimension 0
There are 2 independent parts, one for each index of `ens`. A program takes and returns all parts, laid end to end along the dimension named above; each array names one. Nothing has to cross between parts.
All inputs are finite; a program needn't handle non-finite values.
Results may differ from a plain program's by a relative error of at most 0.0029.
Values may be sent and summed in bfloat16 or wider, within the bound.
A program may use at most 384 MiB of HBM per device.

v0:
```python
import math

import jax
import jax.numpy as jnp
from jax import lax
from jax.sharding import PartitionSpec as P

C = 20
T_SIZE = 4
X = 128
Y = 128
Z = 128
MX = 32
MY = 32
MZ = 32
MT = 2


def centered_modes(mode_count):
    places = jnp.arange(mode_count, dtype=jnp.int32)
    return jnp.where(places < mode_count // 2, places, places - mode_count)


def phase_table(points, frequencies, length):
    product = jnp.remainder(points[:, None] * frequencies[None, :], length)
    return product.astype(jnp.float32) * (2.0 * math.pi / length)


def per_device(frames, counts, spectral_weight, point_weight, point_bias):
    highest = lax.Precision.HIGHEST
    channels, steps_local, x_cells, rows_y, z_cells = frames.shape
    col_index = lax.axis_index("col")
    ta_index = lax.axis_index("ta")
    frame_scale = lax.dynamic_slice_in_dim(counts, ta_index * steps_local, steps_local).astype(
        jnp.float32
    )
    y_points = col_index * rows_y + jnp.arange(rows_y, dtype=jnp.int32)
    y_angles = phase_table(y_points, centered_modes(MY), Y)
    ytable = jnp.concatenate([jnp.cos(y_angles), -jnp.sin(y_angles)], axis=1).astype(jnp.bfloat16)
    z_angles = phase_table(jnp.arange(Z, dtype=jnp.int32), jnp.arange(MZ, dtype=jnp.int32), Z)
    z_table = jnp.concatenate([jnp.cos(z_angles), jnp.sin(z_angles)], axis=1)
    x_angles = phase_table(jnp.arange(X, dtype=jnp.int32), centered_modes(MX), X)
    x_cos = jnp.cos(x_angles)
    x_sin = jnp.sin(x_angles)
    t_points = ta_index * steps_local + jnp.arange(steps_local, dtype=jnp.int32)
    t_angles = phase_table(t_points, jnp.arange(MT, dtype=jnp.int32), T_SIZE)
    time_cos = jnp.cos(t_angles)
    time_sin = jnp.sin(t_angles)
    first = jnp.einsum("ctxyz,yj->ctxjz", frames, ytable, preferred_element_type=jnp.float32)
    second = jnp.einsum("ctxjz,zk->ctxjk", first, z_table, precision=highest)
    real_part = (second[..., :MY, :MZ] + second[..., MY:, MZ:]).reshape(
        channels, steps_local, x_cells, MY * MZ
    )
    imag_part = (second[..., MY:, :MZ] - second[..., :MY, MZ:]).reshape(
        channels, steps_local, x_cells, MY * MZ
    )
    pencils = jnp.stack([real_part, imag_part]) * frame_scale[None, None, :, None, None]
    pencils = lax.psum_scatter(pencils, "col", scatter_dimension=1, tiled=True)
    received = lax.all_to_all(pencils, "gx", split_axis=4, concat_axis=3, tiled=True)
    real_x = jnp.einsum("ntxp,xk->ntkp", received[0], x_cos, precision=highest) + jnp.einsum(
        "ntxp,xk->ntkp", received[1], x_sin, precision=highest
    )
    imag_x = jnp.einsum("ntxp,xk->ntkp", received[1], x_cos, precision=highest) - jnp.einsum(
        "ntxp,xk->ntkp", received[0], x_sin, precision=highest
    )
    real_t = jnp.einsum("ntkp,tm->nmkp", real_x, time_cos, precision=highest) + jnp.einsum(
        "ntkp,tm->nmkp", imag_x, time_sin, precision=highest
    )
    imag_t = jnp.einsum("ntkp,tm->nmkp", imag_x, time_cos, precision=highest) - jnp.einsum(
        "ntkp,tm->nmkp", real_x, time_sin, precision=highest
    )
    kept_modes = jnp.stack([real_t, imag_t])
    input_count = kept_modes.shape[1]
    pencil_share = kept_modes.shape[4]
    mixing = spectral_weight.astype(jnp.float32).reshape(2, C, input_count, pencil_share, MT, MX)
    real_v = jnp.einsum(
        "oipmk,imkp->omkp", mixing[0], kept_modes[0], precision=highest
    ) - jnp.einsum("oipmk,imkp->omkp", mixing[1], kept_modes[1], precision=highest)
    imag_v = jnp.einsum(
        "oipmk,imkp->omkp", mixing[0], kept_modes[1], precision=highest
    ) + jnp.einsum("oipmk,imkp->omkp", mixing[1], kept_modes[0], precision=highest)
    mixed = lax.psum(jnp.stack([real_v, imag_v]), ("ta", "col"))
    g_real = jnp.einsum("omkp,tm->otkp", mixed[0], time_cos, precision=highest) - jnp.einsum(
        "omkp,tm->otkp", mixed[1], time_sin, precision=highest
    )
    g_imag = jnp.einsum("omkp,tm->otkp", mixed[1], time_cos, precision=highest) + jnp.einsum(
        "omkp,tm->otkp", mixed[0], time_sin, precision=highest
    )
    h_real = jnp.einsum("otkp,xk->otxp", g_real, x_cos, precision=highest) - jnp.einsum(
        "otkp,xk->otxp", g_imag, x_sin, precision=highest
    )
    h_imag = jnp.einsum("otkp,xk->otxp", g_imag, x_cos, precision=highest) + jnp.einsum(
        "otkp,xk->otxp", g_real, x_sin, precision=highest
    )
    returned = lax.all_to_all(
        jnp.stack([h_real, h_imag]), "gx", split_axis=3, concat_axis=4, tiled=True
    )
    pencil_grid = returned.reshape(2, C, steps_local, x_cells, MY, MZ)
    z_weight = jnp.where(jnp.arange(MZ, dtype=jnp.int32) == 0, 1.0, 2.0).astype(
        jnp.float32
    ) / float(T_SIZE * X * Y * Z)
    z_cos_inv = jnp.cos(z_angles).T * z_weight[:, None]
    z_sin_inv = jnp.sin(z_angles).T * z_weight[:, None]
    z_real = jnp.einsum(
        "otxjk,kz->otxjz", pencil_grid[0], z_cos_inv, precision=highest
    ) - jnp.einsum("otxjk,kz->otxjz", pencil_grid[1], z_sin_inv, precision=highest)
    z_imag = jnp.einsum(
        "otxjk,kz->otxjz", pencil_grid[1], z_cos_inv, precision=highest
    ) + jnp.einsum("otxjk,kz->otxjz", pencil_grid[0], z_sin_inv, precision=highest)
    stacked = jnp.concatenate([z_real, z_imag], axis=3)
    y_inverse = jnp.concatenate([jnp.cos(y_angles).T, -jnp.sin(y_angles).T], axis=0)
    spectral = jnp.einsum("otxjz,jy->otxyz", stacked, y_inverse, precision=highest)
    pointwise = jnp.einsum(
        "oi,itxyz->otxyz", point_weight, frames, preferred_element_type=jnp.float32
    )
    summed = (
        spectral
        + pointwise * frame_scale[None, :, None, None, None]
        + point_bias[:, None, None, None, None]
    )
    return jax.nn.gelu(summed).astype(jnp.bfloat16)


def solution(mesh):
    return jax.shard_map(
        per_device,
        mesh=mesh,
        in_specs=(
            P("ens", "ta", "gx", "col", None),
            P("ens"),
            P(None, "ens", "col", "gx"),
            P("ens", None),
            P("ens"),
        ),
        out_specs=P("ens", "ta", "gx", "col", None),
        check_vma=False,
    )
```

profile of v0, /device:TPU:0, one launch (start us, length us, event | category | flops | bytes accessed | tf_op | source)
XLA Modules:
  0.0 1330.4 jit_solution(6562111594683278277)
XLA Ops:
  6.8 20.8 %fusion.62 = f32[64,20,2,32,128]{4,0,3,2,1:T(8,128)} fusion(bf16[20,2,32,64,128]{4,3,2,1,0:T(8,128)(2,1)} %param.5, bf16[64,32]{0,1:T(8,128)(2,1)S(1)} %get-tuple-element.20, bf16[64,32]{0,1:T(8,128)(2,1)S(1)} %get-tuple-element.19), kind=kOutput, calls=%fused_computation.110 | convolution fusion | flops 1342193664 | bytes 62922752 | tf_op jit(solution)/shard_map/ctxyz,yj->ctxjz/dot_general | solution.py:49
  27.6 39.3 %fusion.17 = f32[20,2,32,64,64]{4,3,2,1,0:T(8,128)} fusion(f32[64,20,2,32,128]{4,0,3,2,1:T(8,128)} %fusion.62, f32[128,32]{0,1:T(8,128)S(1)} %get-tuple-element.21, f32[128,32]{0,1:T(8,128)S(1)} %get-tuple-element.22), kind=kOutput, calls=%fused_computation.23 | convolution fusion | flops 8053071872 | bytes 62947328 | tf_op jit(solution)/shard_map/ctxjz,zk->ctxjk/dot_general | solution.py:50
  66.9 42.8 %slice_add_fusion = (f32[20,2,32,32,32]{4,3,2,1,0:T(8,128)}, f32[20,2,32,32,32]{4,3,2,1,0:T(8,128)}) fusion(f32[20,2,32,64,64]{4,3,2,1,0:T(8,128)} %fusion.17), kind=kLoop, calls=%fused_computation.29 | loop fusion | flops 2621440 | bytes 31457280 | tf_op jit(solution)/shard_map/add | solution.py:51
  109.7 16.7 %stack_reshape.6 = f32[1,20,2,32,1024]{4,3,2,1,0:T(8,128)} reshape(f32[20,2,32,32,32]{4,3,2,1,0:T(8,128)} %get-tuple-element.9) | data formatting | bytes 10485760 | tf_op jit(solution)/shard_map/stack;reshape | solution.py:57
  126.3 16.9 %stack_reshape.7 = f32[1,20,2,32,1024]{4,3,2,1,0:T(8,128)} reshape(f32[20,2,32,32,32]{4,3,2,1,0:T(8,128)} %get-tuple-element.10) | data formatting | bytes 10485760 | tf_op jit(solution)/shard_map/stack;reshape | solution.py:57
  156.5 43.7 %all-reduce.6.cloned.1.call-done = f32[2,20,2,32,1024]{4,3,2,1,0:T(8,128)} async-done(((f32[2,20,2,32,1024]{4,3,2,1,0:T(8,128)}), f32[2,20,2,32,1024]{4,3,2,1,0:T(8,128)}) %all-reduce.6.cloned.1.call-update) | async-done | bytes 10485776
  205.8 23.6 %copy.39 = f32[2,10,2,32,1024]{3,2,1,0,4:T(2,128)} copy(f32[2,10,2,32,1024]{4,3,2,1,0:T(8,128)} %constant_dynamic-slice_fusion) | data formatting | bytes 10485760 | tf_op jit(solution)/shard_map/reduce_scatter | solution.py:58
  229.4 34.3 %reshape.65 = f32[4,1,327680]{2,1,0:T(1,128)} reshape(f32[1024,2,10,2,32]{4,3,2,1,0:T(2,128)} %bitcast.187) | data formatting | bytes 10485760
  268.9 30.6 %fusion.217 = (bf16[1,20,10,16384]{3,0,2,1:T(2,128)(2,1)}, bf16[1,20,10,16384]{3,0,2,1:T(2,128)(2,1)}) fusion(bf16[2,20,10,16384]{3,0,2,1:T(2,128)(2,1)} %param.7), kind=kLoop, calls=%fused_computation.258 | loop fusion | bytes 26214400 | tf_op jit(solution)/shard_map/slice | solution.py:78
  314.7 21.6 %squeeze.35 = bf16[20,10,256,2,32]{4,3,2,0,1:T(2,128)(2,1)} reshape(bf16[1,20,10,16384]{3,1,2,0:T(8,128)(2,1)} %copy.50) | data formatting | bytes 13107200 | tf_op jit(solution)/shard_map/squeeze | solution.py:78
  351.7 21.5 %squeeze.34 = bf16[20,10,256,2,32]{4,3,2,0,1:T(2,128)(2,1)} reshape(bf16[1,20,10,16384]{3,1,2,0:T(8,128)(2,1)} %copy.45) | data formatting | bytes 13107200 | tf_op jit(solution)/shard_map/squeeze | solution.py:77
  385.9 18.6 %reduce.8 = f32[4,327680]{1,0:T(4,128)} reduce(f32[4,1,327680]{2,1,0:T(1,128)} %all-to-all-done, f32[]{:T(128)} %broadcast.278), dimensions={1}, to_apply=%all_to_all.22.reduce_sub_computation | reduce | bytes 10485764 | tf_op jit(solution)/shard_map/all_to_all | solution.py:59
  404.5 37.8 %reshape.66 = f32[1024,2,10,2,32]{4,3,2,1,0:T(2,128)} reshape(f32[4,327680]{1,0:T(4,128)} %reduce.8) | data formatting | bytes 10485760
  442.3 24.2 %copy.40 = f32[2,10,2,32,4,256]{5,3,4,2,1,0:T(8,128)} copy(f32[2,10,2,32,4,256]{3,2,1,0,5,4:T(2,128)} %bitcast.188) | data formatting | bytes 10485760 | tf_op jit(solution)/shard_map/all_to_all | solution.py:59
  500.6 106.9 %fusion.2 = (f32[2,32,256,20]{1,0,2,3:T(2,128)}, f32[2,32,256,20]{1,0,2,3:T(2,128)}) fusion(f32[2,32,256,10]{1,0,2,3:T(2,128)S(1)} %copy.112, bf16[20,10,256,2,32]{4,3,2,0,1:T(2,128)(2,1)} %squeeze.35, f32[2,32,256,10]{1,0,2,3:T(2,128)} %copy.111), kind=kLoop, calls=%fused_computation.7 | loop fusion | flops 15728640 | bytes 10485760
  615.1 105.9 %fusion = (f32[2,32,256,20]{1,0,2,3:T(2,128)}, f32[2,32,256,20]{1,0,2,3:T(2,128)}) fusion(f32[2,32,256,10]{1,0,2,3:T(2,128)} %copy.111, bf16[20,10,256,2,32]{4,3,2,0,1:T(2,128)(2,1)} %squeeze.34, f32[2,32,256,10]{1,0,2,3:T(2,128)S(1)} %copy.112), kind=kLoop, calls=%fused_computation.5 | loop fusion | flops 15728640 | bytes 10485760
  749.5 59.3 %all-reduce.4.cloned.1.call-done = f32[2,20,2,32,256]{4,2,3,1,0:T(2,128)} async-done(((f32[2,20,2,32,256]{4,2,3,1,0:T(2,128)}), f32[2,20,2,32,256]{4,2,3,1,0:T(2,128)}) %all-reduce.4.cloned.1.call-update) | async-done | bytes 2621456 | tf_op jit(solution)/shard_map/psum | solution.py:82
  880.3 31.0 %fusion.19 = f32[20,2,32,64,128]{4,0,3,2,1:T(8,128)} fusion(bf16[20,2,32,64,128]{4,3,2,1,0:T(8,128)(2,1)} %param.5, bf16[20,20]{1,0:T(8,128)(2,1)S(1)} %copy-done), kind=kOutput, calls=%fused_computation.26 | convolution fusion | flops 419430400 | bytes 62915360 | tf_op jit(solution)/shard_map/oi,itxyz->otxyz/dot_general | solution.py:113
  911.3 197.0 %all-to-all-done.1 = f32[2,20,2,128,256]{4,2,1,0,3:T(2,128)} async-done(((f32[2,20,2,128,256]{4,2,1,0,3:T(2,128)}), f32[2,20,2,128,256]{4,2,1,0,3:T(2,128)}, u32[]{:S(2)}, u32[]{:S(2)}) %all-to-all-start.1) | async-done | bytes 10485792 | tf_op jit(solution)/shard_map/all_to_all | solution.py:95
  1162.1 22.2 %fusion.69 = f32[20,2,32,32,128]{4,3,2,1,0:T(8,128)} fusion(f32[20,2,32,32,32]{4,3,2,1,0:T(8,128)} %squeeze.38, f32[32]{0:T(128)S(1)} %fusion.123), kind=kOutput, calls=%fused_computation.117 | convolution fusion | flops 2013327360 | bytes 26214528 | tf_op jit(solution)/shard_map/otxjk,kz->otxjz/dot_general | solution.py:104
  1184.3 22.2 %fusion.67 = f32[20,2,32,32,128]{4,3,2,1,0:T(8,128)} fusion(f32[20,2,32,32,32]{4,3,2,1,0:T(8,128)} %squeeze.39, f32[32]{0:T(128)S(1)} %fusion.123), kind=kOutput, calls=%fused_computation.115 | convolution fusion | flops 2013327360 | bytes 26214528 | tf_op jit(solution)/shard_map/otxjk,kz->otxjz/dot_general | solution.py:107
  1206.5 30.0 %convolution_subtract_fusion = f32[20,2,32,32,128]{4,3,2,1,0:T(8,128)} fusion(f32[20,2,32,32,128]{4,3,2,1,0:T(8,128)} %fusion.69, f32[20,2,32,32,32]{4,3,2,1,0:T(8,128)} %squeeze.39, f32[32]{0:T(128)S(1)} %fusion.123), kind=kOutput, calls=%fused_computation.34 | convolution fusion | flops 2018570240 | bytes 47186048 | tf_op jit(solution)/shard_map/otxjk,kz->otxjz/dot_general | solution.py:106
  1236.5 22.3 %convolution_add_fusion = f32[20,2,32,32,128]{4,3,2,1,0:T(8,128)} fusion(f32[20,2,32,32,128]{4,3,2,1,0:T(8,128)} %fusion.67, f32[20,2,32,32,32]{4,3,2,1,0:T(8,128)S(1)} %bitcast.186, f32[32]{0:T(128)S(1)} %fusion.123), kind=kOutput, calls=%fused_computation.33 | convolution fusion | flops 2018570240 | bytes 47186048 | tf_op jit(solution)/shard_map/otxjk,kz->otxjz/dot_general | solution.py:109
  1258.8 64.3 %fusion.11 = bf16[20,2,32,64,128]{4,3,2,1,0:T(8,128)(2,1)} fusion(f32[20,2,32,64,128]{4,0,3,2,1:T(8,128)} %fusion.19, f32[20]{0:T(128)S(1)} %copy-done.11, f32[2]{0:T(128)S(1)} %copy-done.9, f32[20,2,32,32,128]{4,3,2,1,0:T(8,128)} %convolution_add_fusion, f32[20,2,32,32,128]{4,3,2,1,0:T(8,128)} %convolution_subtract_fusion, ...), kind=kOutput, calls=%fused_computation.16 | convolution fusion | flops 8189382656 | bytes 104874072 | tf_op jit(solution)/shard_map/otxjz,jy->otxyz/dot_general | solution.py:112
  (90 shorter events, 262.3 us)
Async XLA Ops:
  6.5 873.8 %copy-start = (bf16[20,20]{1,0:T(8,128)(2,1)S(1)}, bf16[20,20]{1,0:T(8,128)(2,1)}, u32[]{:S(2)}) copy-start(bf16[20,20]{1,0:T(8,128)(2,1)} %param.8) | copy-start | bytes 2404
  6.5 193.6 %all-reduce.6.cloned.1.call-start = ((), (), s32[]{:S(2)}) async-start(), calls=%async_computation.3 | async-start | bytes 20971520
  6.5 21.1 %copy-start.4 = (s32[32]{0:T(128)}, s32[32]{0:T(128)S(1)}, u32[]{:S(2)}) copy-start(s32[32]{0:T(128)S(1)} %compare_select_fusion) | copy-start | bytes 388
  6.7 21.0 %copy-start.6 = (s32[64]{0:T(128)}, s32[64]{0:T(128)S(1)}, u32[]{:S(2)}) copy-start(s32[64]{0:T(128)S(1)} %iota_add_fusion.1) | copy-start | bytes 772
  126.3 16.9 %copy-start.10 = (s32[4]{0:T(128)S(1)}, s32[4]{0:T(128)}, u32[]{:S(2)}) copy-start(s32[4]{0:T(128)} %param.6) | copy-start | bytes 52
  143.3 0.6 copy-start.8
  154.6 0.7 copy-start.12
  263.8 121.6 %all-to-all-start = ((f32[4,1,327680]{2,1,0:T(1,128)}), f32[4,1,327680]{2,1,0:T(1,128)}, u32[]{:S(2)}, u32[]{:S(2)}) async-start(f32[4,1,327680]{2,1,0:T(1,128)} %reshape.65), calls=%async_computation | async-start | bytes 10485760 | tf_op jit(solution)/shard_map/all_to_all | solution.py:59
  268.8 540.0 %all-reduce.4.cloned.1.call-start = ((), (), s32[]{:S(2)}) async-start(), calls=%async_computation.2 | async-start | bytes 5242880 | tf_op jit(solution)/shard_map/psum | solution.py:82
  466.5 3.0 copy-start.5
  727.6 16.0 %copy-start.2 = (f32[2,32,256,20]{2,0,1,3:T(2,128)S(1)}, f32[2,32,256,20]{2,0,1,3:T(2,128)}, u32[]{:S(2)}) copy-start(f32[2,32,256,20]{2,0,1,3:T(2,128)} %copy.82) | copy-start | bytes 3932164
  808.8 17.5 %copy-start.3 = (f32[2,20,2,32,256]{4,2,3,1,0:T(2,128)S(1)}, f32[2,20,2,32,256]{4,2,3,1,0:T(2,128)}, u32[]{:S(2)}) copy-start(f32[2,20,2,32,256]{4,2,3,1,0:T(2,128)} %all-reduce.4.cloned.1.call-done) | copy-start | bytes 7864324
  873.6 6.5 copy-start.7
  873.6 234.7 %all-to-all-start.1 = ((f32[2,20,2,128,256]{4,2,1,0,3:T(2,128)}), f32[2,20,2,128,256]{4,2,1,0,3:T(2,128)}, u32[]{:S(2)}, u32[]{:S(2)}) async-start(f32[2,20,2,128,256]{4,2,1,0,3:T(2,128)} %copy.55), calls=%async_computation.1 | async-start | bytes 20971520 | tf_op jit(solution)/shard_map/all_to_all | solution.py:95
  1184.3 52.2 %slice-start = ((s8[20971520]{0:T(1024)(128)(4,1)}), s8[4194304]{0:T(1024)(128)(4,1)S(1)}, s32[]{:S(2)}) async-start(s8[20971520]{0:T(1024)(128)(4,1)} %bitcast.185), calls=%async_computation.4 | async-start | bytes 8388608
  1184.3 52.2 %slice-start.1 = ((s8[20971520]{0:T(1024)(128)(4,1)}), s8[4194304]{0:T(1024)(128)(4,1)S(1)}, s32[]{:S(2)}) async-start(s8[20971520]{0:T(1024)(128)(4,1)} %bitcast.185), calls=%async_computation.5 | async-start | bytes 8388608
  1206.5 30.0 %slice-start.2 = ((s8[20971520]{0:T(1024)(128)(4,1)}), s8[4194304]{0:T(1024)(128)(4,1)S(1)}, s32[]{:S(2)}) async-start(s8[20971520]{0:T(1024)(128)(4,1)} %bitcast.185), calls=%async_computation.6 | async-start | bytes 8388608
  1206.5 30.0 %slice-start.3 = ((s8[20971520]{0:T(1024)(128)(4,1)}), s8[4194304]{0:T(1024)(128)(4,1)S(1)}, s32[]{:S(2)}) async-start(s8[20971520]{0:T(1024)(128)(4,1)} %bitcast.185), calls=%async_computation.7 | async-start | bytes 8388608
  1206.5 30.0 %slice-start.4 = ((s8[20971520]{0:T(1024)(128)(4,1)}), s8[4194304]{0:T(1024)(128)(4,1)S(1)}, s32[]{:S(2)}) async-start(s8[20971520]{0:T(1024)(128)(4,1)} %bitcast.185), calls=%async_computation.8 | async-start | bytes 8388608
  1236.5 22.3 %copy-start.9 = (f32[2]{0:T(128)S(1)}, f32[2]{0:T(128)}, u32[]{:S(2)}) copy-start(f32[2]{0:T(128)} %copy-done.8) | copy-start | bytes 28
  1236.5 22.3 %copy-start.11 = (f32[20]{0:T(128)S(1)}, f32[20]{0:T(128)}, u32[]{:S(2)}) copy-start(f32[20]{0:T(128)} %param.9) | copy-start | bytes 244
  1258.8 64.3 %copy-start.1 = (bf16[20,20]{1,0:T(8,128)(2,1)S(1)}, bf16[20,20]{1,0:T(8,128)(2,1)}, u32[]{:S(2)}) copy-start(bf16[20,20]{1,0:T(8,128)(2,1)} %param.8) | copy-start | bytes 2404
Sparse Core Ops, SparseCore 0:
  154.7 45.3 all-reduce.5
  749.6 59.1 all-reduce.3
where the time goes:
time: 1340 us; the launch traced here: 1330 us
  local copies, waits for them, and re-layouts  376 us (28%)
  matrix products  320 us (24%)
  waiting for transfers between devices  312 us (23%)
  other arithmetic  296 us (22%)
  between operations  14.8 us (1%)
    unnamed x3, other arithmetic  213 us
    all_to_all x1, waiting for transfers between devices, per_device(): lax.all_to_all(jnp.stack([h_real, h_imag]), 'gx', split_axis=3, concat_ax...  197 us
    unnamed x42, local copies, waits for them, and re-layouts  87.6 us
    dot_general x1, matrix products, per_device(): jnp.einsum('otxjz,jy->otxyz', stacked, y_inverse, precision=highest)  64.3 us
    psum x1, waiting for transfers between devices, per_device(): mixed = lax.psum(jnp.stack([real_v, imag_v]), ('ta', 'col'))  59.3 us
    slice x2, local copies, waits for them, and re-layouts, per_device(): mixing[1]  45.8 us
    unnamed x3, waiting for transfers between devices  43.7 us
    add x1, other arithmetic, per_device(): second[..., :MY, :MZ] + second[..., MY:, MZ:]  42.8 us
  transfers between devices with their start and end apart: 4, of which 4 were waited for; matrix products, arithmetic and copies ran while one was open for 10% of the time, Pallas kernels for 0%

commit v1 on v0

v1 whole, which is shorter than its diff:
```python
import functools

import jax
import jax.numpy as jnp
import numpy as np
from jax import lax
from jax.experimental import pallas as pl
from jax.experimental.pallas import tpu as pltpu
from jax.sharding import PartitionSpec as P

MX = 32
MY = 32
MZ = 32
MT = 2
PACK = 4
F32 = jnp.float32
BF16 = jnp.bfloat16


def centered(count):
    places = np.arange(count)
    return np.where(places < count // 2, places, places - count)


def angles(points, frequencies, length):
    return (np.outer(points, frequencies) % length) * (2.0 * np.pi / length)


def split(value):
    high = value.astype(BF16)
    return high, (value - high.astype(F32)).astype(BF16)


def dot(a, b):
    return jnp.dot(a, b, preferred_element_type=F32)


def forward_kernel(steps, rows_y, f_ref, z_ref, y_ref, x_ref, out_ref, held):
    at_once = 4 if steps % 4 == 0 else 1

    def cells(block, carry):
        base = block * at_once
        wide = jnp.concatenate(
            [
                f_ref[c, 0, pl.ds(base, at_once)].reshape(at_once * rows_y, f_ref.shape[-1])
                for c in range(PACK)
            ],
            axis=1,
        )
        g = dot(wide, z_ref[0]) + dot(wide, z_ref[1])
        for s in range(at_once):
            part = g[s * rows_y : (s + 1) * rows_y]
            pair = jnp.concatenate([part[:, : PACK * MZ], part[:, PACK * MZ :]], axis=0)
            high, low = split(pair)
            held[pl.ds(pl.multiple_of((base + s) * 2 * MY, 2 * MY), 2 * MY), :] = dot(
                y_ref[...], jnp.concatenate([high, low], axis=0)
            )
        return carry

    lax.fori_loop(0, steps // at_once, cells, 0)
    half = PACK * MZ // 2
    lane = lax.broadcasted_iota(jnp.int32, (MT * MX, PACK * MZ), 1)

    def modes(ky, carry):
        real = held[pl.ds(ky, steps, stride=2 * MY), :]
        imag = held[pl.ds(ky + MY, steps, stride=2 * MY), :]
        high, low = split(jnp.concatenate([real, imag], axis=0))
        m = dot(x_ref[0], high) + dot(x_ref[0], low) + dot(x_ref[1], high)
        m_real, m_imag = m[: MT * MX], m[MT * MX :]
        out_ref[0, 0, ky] = jnp.where(lane < half, m_real, pltpu.roll(m_imag, half, 1))
        out_ref[1, 0, ky] = jnp.where(lane < half, pltpu.roll(m_real, half, 1), m_imag)
        return carry

    lax.fori_loop(0, MY, modes, 0, unroll=2)


def mixing_kernel(outputs, w_ref, m_ref, out_ref):
    m_real, m_imag = m_ref[0], m_ref[1]
    for o in range(outputs):
        w_real = w_ref[0, o].astype(F32)
        w_imag = w_ref[1, o].astype(F32)
        out_ref[0, pl.ds(o, 1), :] = jnp.sum(
            w_real * m_real - w_imag * m_imag, axis=0, keepdims=True
        )
        out_ref[1, pl.ds(o, 1), :] = jnp.sum(
            w_real * m_imag + w_imag * m_real, axis=0, keepdims=True
        )


def inverse_kernel(
    steps, groups, rows_y, m_ref, f_ref, x_ref, y_ref, z_ref, p_ref, c_ref, b_ref, out_ref, held, spec
):
    half = PACK * MZ // 2
    parts, kys = m_ref.shape[0], m_ref.shape[3]
    x_block = f_ref.shape[2]
    z_cells = f_ref.shape[4]
    channels = groups * PACK
    t_now, x_now = pl.program_id(0), pl.program_id(1)

    @pl.when(jnp.logical_and(t_now == 0, x_now == 0))
    def _():
        lane = lax.broadcasted_iota(jnp.int32, (MT * MX, PACK * MZ), 1)

        def one(index, carry):
            part = index // kys
            k = index % kys
            ky = index
            for g in range(groups):
                first = m_ref[part, 0, g, k].astype(F32)
                second = m_ref[part, 1, g, k].astype(F32)
                real = jnp.where(lane < half, first, pltpu.roll(second, half, 1))
                imag = jnp.where(lane < half, pltpu.roll(first, half, 1), second)
                high, low = split(jnp.concatenate([real, imag], axis=0))
                h = dot(x_ref[0], high) + dot(x_ref[0], low) + dot(x_ref[1], high)
                held[g, pl.ds(ky * steps, steps), :] = h[:steps]
                held[g, pl.ds((ky + MY) * steps, steps), :] = h[steps:]
            return carry

        lax.fori_loop(0, parts * kys, one, 0)

    scale = c_ref[t_now]

    def cell(x, carry):
        tx = (t_now * pl.num_programs(1) + x_now) * x_block + x
        for g in range(groups):
            high, low = split(held[g, pl.ds(tx, 2 * MY, stride=steps), :])
            d = dot(y_ref[0], high) + dot(y_ref[0], low) + dot(y_ref[1], high)
            wide = jnp.concatenate([d[:rows_y], d[rows_y:]], axis=1)
            high, low = split(wide)
            s = dot(high, z_ref[0]) + dot(low, z_ref[0]) + dot(high, z_ref[1])
            for u in range(PACK):
                spec[u * groups + g] = s[:, u * z_cells : (u + 1) * z_cells]
        for y in range(0, rows_y, 32):
            both = jnp.concatenate(
                [
                    f_ref[:, 0, x, y + 16 * s : y + 16 * (s + 1), :].reshape(channels * 16, z_cells)
                    for s in range(2)
                ],
                axis=1,
            )
            point = dot(p_ref[...], both) * scale
            for c in range(channels):
                for s in range(2):
                    low_y = y + 16 * s
                    v = (
                        spec[c, low_y : low_y + 16, :]
                        + point[c * 16 : (c + 1) * 16, s * z_cells : (s + 1) * z_cells]
                        + b_ref[c]
                    )
                    inner = v * (0.7978845608028654 + 0.035677408136300125 * (v * v))
                    hv = 0.5 * v
                    out_ref[c, 0, x, low_y : low_y + 16, :] = (hv + hv * jnp.tanh(inner)).astype(
                        out_ref.dtype
                    )
        return carry

    lax.fori_loop(0, x_block, cell, 0)


def per_device(sizes, frames, counts, spectral_weight, point_weight, point_bias):
    gx_size, ta_size, col_size = sizes
    channels, t_local, x_local, rows_y, z_cells = frames.shape
    t_size, x_size, y_size = t_local * ta_size, x_local * gx_size, rows_y * col_size
    groups = channels // PACK
    steps = t_local * x_local
    ky_share = MY // gx_size
    lanes = PACK * MZ
    col = lax.axis_index("col")
    ta = lax.axis_index("ta")
    gx = lax.axis_index("gx")
    vmem = 56 * 1024 * 1024

    z_ang = angles(np.arange(z_cells), np.arange(MZ), z_cells)
    eye = np.eye(PACK)
    z_fwd = np.concatenate([np.kron(eye, np.cos(z_ang)), np.kron(eye, np.sin(z_ang))], axis=1)
    z_fwd = jnp.stack(split(jnp.asarray(z_fwd, F32)))
    weight = np.where(np.arange(MZ) == 0, 1.0, 2.0)[:, None] / float(
        t_size * x_size * y_size * z_cells
    )
    z_inv = np.concatenate(
        [np.kron(eye, np.cos(z_ang).T * weight), np.kron(eye, -np.sin(z_ang).T * weight)], axis=0
    )
    z_inv = jnp.stack(split(jnp.asarray(z_inv, F32)))
    y_ang = angles(np.arange(y_size), centered(MY), y_size)
    y_cos, y_sin = np.cos(y_ang).T, np.sin(y_ang).T
    y_fwd = jnp.asarray(np.stack([np.stack([y_cos, -y_sin], 1), np.stack([-y_sin, -y_cos], 1)]), F32)
    y_fwd = lax.dynamic_slice_in_dim(y_fwd, col * rows_y, rows_y, 3).astype(BF16)
    y_fwd = y_fwd.reshape(2 * MY, 2 * rows_y)
    y_fwd = jnp.concatenate([y_fwd, y_fwd], axis=1)
    y_inv = jnp.asarray(
        np.stack([np.stack([y_cos.T, -y_sin.T], 1), np.stack([y_sin.T, y_cos.T], 1)]), F32
    )
    y_inv = lax.dynamic_slice_in_dim(y_inv, col * rows_y, rows_y, 1).reshape(2 * rows_y, 2 * MY)
    y_inv = jnp.stack(split(y_inv))
    x_ang = angles(np.arange(x_size), centered(MX), x_size).T
    t_ang = angles(np.arange(t_size), np.arange(MT), t_size).T
    tx_ang = t_ang[:, None, :, None] + x_ang[None, :, None, :]
    tx = jnp.asarray(np.stack([np.cos(tx_ang), np.sin(tx_ang)]), F32)
    tx = lax.dynamic_slice(
        tx,
        (0, 0, 0, ta * t_local, gx * x_local),
        (2, MT, MX, t_local, x_local),
    ).reshape(2, MT * MX, t_local, x_local)
    frame_scale = lax.dynamic_slice_in_dim(counts, ta * t_local, t_local).astype(F32)
    scaled = (tx * frame_scale[None, None, :, None]).reshape(2, MT * MX, steps)
    x_fwd = jnp.concatenate(
        [
            jnp.concatenate([scaled[0], scaled[1]], axis=1),
            jnp.concatenate([-scaled[1], scaled[0]], axis=1),
        ],
        axis=0,
    )
    x_fwd = jnp.stack(split(x_fwd))
    tx = tx.reshape(2, MT * MX, steps)
    x_inv = jnp.concatenate(
        [
            jnp.concatenate([tx[0].T, -tx[1].T], axis=1),
            jnp.concatenate([tx[1].T, tx[0].T], axis=1),
        ],
        axis=0,
    )
    x_inv = jnp.stack(split(x_inv))
    point_table = jnp.kron(point_weight.astype(F32), jnp.eye(16, dtype=F32)).astype(BF16)

    whole = lambda *shape: pl.BlockSpec(shape, lambda *_: (0,) * len(shape))
    partial = pl.pallas_call(
        functools.partial(forward_kernel, steps, rows_y),
        grid=(groups,),
        in_specs=[
            pl.BlockSpec((PACK, 1, steps, rows_y, z_cells), lambda g: (0, g, 0, 0, 0)),
            whole(*z_fwd.shape),
            whole(*y_fwd.shape),
            whole(*x_fwd.shape),
        ],
        out_specs=pl.BlockSpec((2, 1, MY, MT * MX, lanes), lambda g: (0, g, 0, 0, 0)),
        out_shape=jax.ShapeDtypeStruct((2, groups, MY, MT * MX, lanes), F32),
        scratch_shapes=[pltpu.VMEM((steps * 2 * MY, lanes), F32)],
        compiler_params=pltpu.CompilerParams(vmem_limit_bytes=vmem),
    )(frames.reshape(PACK, groups, steps, rows_y, z_cells), z_fwd, y_fwd, x_fwd)

    swap = [(0, 1), (1, 0)]
    mine = lax.dynamic_index_in_dim(partial, col, 0, keepdims=False)
    other = lax.dynamic_index_in_dim(partial, 1 - col, 0, keepdims=False)
    mine = (mine + lax.ppermute(other, "col", swap)).astype(BF16)
    mine = mine.reshape(groups, gx_size, ky_share, MT * MX, lanes).transpose(1, 0, 2, 3, 4)
    received = lax.all_to_all(mine, "gx", split_axis=0, concat_axis=0, tiled=True)
    modes = jnp.sum(received.astype(F32), axis=0)
    modes = lax.psum(modes, "ta")

    inputs = channels // 2
    flat = ky_share * MZ * MT * MX
    modes = modes.reshape(groups, ky_share, MT * MX, 2, 2, MZ).transpose(3, 4, 0, 1, 5, 2)
    modes = modes.reshape(2, inputs, flat)
    block = min(flat, 2048)
    mixed = pl.pallas_call(
        functools.partial(mixing_kernel, channels),
        grid=(flat // block,),
        in_specs=[
            pl.BlockSpec((2, channels, inputs, block), lambda q: (0, 0, 0, q)),
            pl.BlockSpec((2, inputs, block), lambda q: (0, 0, q)),
        ],
        out_specs=pl.BlockSpec((2, channels, block), lambda q: (0, 0, q)),
        out_shape=jax.ShapeDtypeStruct((2, channels, flat), F32),
        compiler_params=pltpu.CompilerParams(vmem_limit_bytes=vmem),
    )(spectral_weight, modes)

    mixed = mixed.reshape(2, 2, 2, groups, ky_share, MZ, MT * MX).transpose(1, 3, 4, 6, 0, 2, 5)
    mixed = mixed.reshape(2, groups, ky_share, MT * MX, lanes)
    mine = lax.dynamic_index_in_dim(mixed, col, 0, keepdims=False)
    other = lax.dynamic_index_in_dim(mixed, 1 - col, 0, keepdims=False)
    mine = mine + lax.ppermute(other, "col", swap)
    every = lax.all_gather(mine, ("gx", "col"), axis=0, tiled=False)
    every = every.reshape(gx_size, 2, groups, ky_share, MT * MX, lanes)

    x_block = min(x_local, 4)
    frame_spec = pl.BlockSpec(
        (channels, 1, x_block, rows_y, z_cells), lambda t, x: (0, t, x, 0, 0)
    )
    smem = pl.BlockSpec(memory_space=pltpu.SMEM)
    return pl.pallas_call(
        functools.partial(inverse_kernel, steps, groups, rows_y),
        grid=(t_local, x_local // x_block),
        in_specs=[
            pl.BlockSpec(every.shape, lambda t, x: (0,) * 6, pipeline_mode=pl.Buffered(1)),
            frame_spec,
            whole(*x_inv.shape),
            whole(*y_inv.shape),
            whole(*z_inv.shape),
            whole(*point_table.shape),
            smem,
            smem,
        ],
        out_specs=frame_spec,
        out_shape=jax.ShapeDtypeStruct(frames.shape, BF16),
        scratch_shapes=[
            pltpu.VMEM((groups, 2 * MY * steps, lanes), F32),
            pltpu.VMEM((channels, rows_y, z_cells), F32),
        ],
        compiler_params=pltpu.CompilerParams(vmem_limit_bytes=vmem),
    )(every, frames, x_inv, y_inv, z_inv, point_table, frame_scale, point_bias)


def solution(mesh):
    sizes = (mesh.shape["gx"], mesh.shape["ta"], mesh.shape["col"])
    return jax.shard_map(
        functools.partial(per_device, sizes),
        mesh=mesh,
        in_specs=(
            P("ens", "ta", "gx", "col", None),
            P("ens"),
            P(None, "ens", "col", "gx"),
            P("ens", None),
            P("ens"),
        ),
        out_specs=P("ens", "ta", "gx", "col", None),
        check_vma=False,
    )
```

time: 1340 us -> 497 us (0.37)
  local copies, waits for them, and re-layouts: 376 us -> 55.8 us
  matrix products: 320 us -> 0 us
  other arithmetic: 296 us -> 13.9 us
  Pallas kernels: 0 us -> 198 us
  waiting for transfers between devices: 312 us -> 148 us
  blocking collectives: 0 us -> 65.8 us
    dot_general x24 -> x0, matrix products: 320 us -> none  [the longest x1 64.3 us: per_device(): jnp.einsum('otxjz,jy->otxyz', stacked, y_inverse, precision=highest)]
    unnamed x3 -> x0, other arithmetic: 213 us -> none
    all_to_all x2 -> x0, waiting for transfers between devices: 209 us -> none  [the longest x1 197 us: per_device(): lax.all_to_all(jnp.stack([h_real, h_imag]), 'gx', split_axis=3, concat_ax...]
    pallas_call x0 -> x3, Pallas kernels: none -> 198 us  [the longest x1 111 us: per_device(): pl.pallas_call(functools.partial(inverse_kernel, steps, groups, rows_y),...]
    all_gather x0 -> x1, waiting for transfers between devices: none -> 94.3 us  [per_device(): every = lax.all_gather(mine, ('gx', 'col'), axis=0, tiled=False)]
    slice x5 -> x2, local copies, waits for them, and re-layouts: 75.6 us -> 0.9 us  [the longest x1 0.9 us: per_device(): tx[1]]
    unnamed x42 -> x7, local copies, waits for them, and re-layouts: 87.6 us -> 18.8 us
    all_to_all x0 -> x1, blocking collectives: none -> 65.8 us  [per_device(): lax.all_to_all(mine, 'gx', split_axis=0, concat_axis=0, tiled=True)]
  transfers between devices with their start and end apart: 4 -> 4, of which waited for: 4 -> 4; matrix products, arithmetic and copies ran while one was open for 10% -> 5% of each run, Pallas kernels for 0% -> 0%
where the time goes in v1:
time: 497 us; the launch traced here: 496 us
  Pallas kernels  198 us (40%)
  waiting for transfers between devices  148 us (30%)
  blocking collectives  65.8 us (13%)
  local copies, waits for them, and re-layouts  55.8 us (11%)
  other arithmetic  13.9 us (3%)
  between operations  13.6 us (3%)
    pallas_call x1, Pallas kernels, per_device(): pl.pallas_call(functools.partial(inverse_kernel, steps, groups, rows_y),...  111 us
    all_gather x1, waiting for transfers between devices, per_device(): every = lax.all_gather(mine, ('gx', 'col'), axis=0, tiled=False)  94.3 us
    pallas_call x1, Pallas kernels, per_device(): pl.pallas_call(functools.partial(forward_kernel, steps, rows_y), grid=(gr...  69.9 us
    all_to_all x1, blocking collectives, per_device(): lax.all_to_all(mine, 'gx', split_axis=0, concat_axis=0, tiled=True)  65.8 us
    psum x1, waiting for transfers between devices, per_device(): modes = lax.psum(modes, 'ta')  43.1 us
    unnamed x7, local copies, waits for them, and re-layouts  18.8 us
    pallas_call x1, Pallas kernels, per_device(): pl.pallas_call(functools.partial(mixing_kernel, channels), grid=(flat //...  16.9 us
  transfers between devices with their start and end apart: 4, of which 4 were waited for; matrix products, arithmetic and copies ran while one was open for 5% of the time, Pallas kernels for 0%

profile of v1, /device:TPU:0, one launch (start us, length us, event | category | flops | bytes accessed | tf_op | source)
XLA Modules:
  0.0 495.6 jit_solution(2917955142987179091)
XLA Ops:
  7.3 0.9 constant_dynamic-slice_fusion.5
  10.9 69.9 %shard_map.100 = f32[2,5,32,64,128]{4,3,2,1,0:T(8,128)} custom-call(bf16[4,5,64,64,128]{4,3,2,1,0:T(8,128)(2,1)} %bitcast.44, bf16[2,512,256]{2,1,0:T(8,128)(2,1)} %constant.62.z_ref, bf16[64,256]{1,0:T(8,128)(2,1)} %pad_maximum_fusion.5.y_ref, bf16[2,128,128]{2,1,0:T(8,128)(2,1)} %pad_maximum_fusion.1.x_ref), custom_call_target="tpu_custom_call" | custom-call | tf_op jit(solution)/shard_map/pallas_call | solution.py:226
  80.8 5.6 %dynamic-slice_bitcast_fusion = f32[5,32,64,128]{3,2,1,0:T(8,128)} fusion(f32[2,5,32,64,128]{4,3,2,1,0:T(8,128)} %shard_map.100, s32[]{:T(128)S(6)} %select_n.25), kind=kLoop, calls=%fused_computation.3 | loop fusion | bytes 10485764 | tf_op jit(solution)/shard_map/jit(dynamic_index_in_dim)/squeeze | solution.py:243
  86.9 8.6 %collective-permute-done = f32[5,32,64,128]{3,2,1,0:T(8,128)} collective-permute-done((f32[5,32,64,128]{3,2,1,0:T(8,128)}, f32[5,32,64,128]{3,2,1,0:T(8,128)}, u32[]{:S(2)}, u32[]{:S(2)}) %collective-permute-start) | collective-permute-done | bytes 5242912 | tf_op jit(solution)/shard_map/ppermute | solution.py:244
  95.5 5.4 %fusion = bf16[5,32,64,128]{3,2,1,0:T(8,128)(2,1)S(1)} fusion(f32[5,32,64,128]{3,2,1,0:T(8,128)} %collective-permute-done, f32[2,5,32,64,128]{4,3,2,1,0:T(8,128)} %shard_map.100, s32[]{:T(128)S(6)} %select_n.24), kind=kLoop, calls=%fused_computation.1 | loop fusion | flops 2621440 | bytes 13107204 | tf_op jit(solution)/shard_map/convert_element_type | solution.py:244
  101.5 65.8 %all_to_all.5 = bf16[4,5,8,64,128]{4,3,2,1,0:T(8,128)(2,1)S(1)} all-to-all(bf16[4,5,8,64,128]{4,3,2,1,0:T(8,128)(2,1)S(1)} %copy.71), channel_id=1, replica_groups=mesh['ens'=2,'gx'=4,'ta'=2,'col'=2] {'gx'}, dimensions={0} | all-to-all | bytes 5242880 | tf_op jit(solution)/shard_map/all_to_all | solution.py:246
  167.2 1.6 convert_reduce_fusion
  168.8 1.9 copy.73
  170.7 1.8 copy.84
  172.6 3.2 reshape.236
  176.1 18.8 %copy.76.w_ref = bf16[2,20,10,16384]{3,2,1,0:T(8,128)(2,1)} copy(bf16[2,20,10,16384]{3,0,2,1:T(2,128)(2,1)} %param.12) | data formatting | bytes 26214400 | tf_op args[2]
  194.9 43.1 %all-reduce.2.cloned.1.call-done.m_ref = f32[2,10,16384]{2,1,0:T(8,128)} async-done(((f32[2,10,16384]{2,1,0:T(8,128)}), f32[2,10,16384]{2,1,0:T(8,128)}) %all-reduce.2.cloned.1.call-update) | async-done | bytes 1310736 | tf_op jit(solution)/shard_map/psum | solution.py:248
  238.0 16.9 %shard_map.101 = f32[2,20,16384]{2,1,0:T(8,128)} custom-call(bf16[2,20,10,16384]{3,2,1,0:T(8,128)(2,1)} %copy.76.w_ref, f32[2,10,16384]{2,1,0:T(8,128)} %all-reduce.2.cloned.1.call-done.m_ref), custom_call_target="tpu_custom_call" | custom-call | tf_op jit(solution)/shard_map/pallas_call | solution.py:255
  254.9 3.9 copy.77
  258.9 4.4 reshape.230
  263.3 3.1 copy.78
  266.4 2.0 constant_dynamic-slice_fusion.4
  268.4 3.0 copy.80
  271.4 1.8 copy.79
  273.2 1.6 collective-permute-done.1
  274.7 3.0 bitcast_add_fusion.1
  279.8 1.8 convert_element_type.169.p_ref
  283.0 94.3 %all-gather.3.cloned.1.call-done = f32[40,8,64,128]{3,2,1,0:T(8,128)} async-done(((f32[5,8,64,128]{3,2,1,0:T(8,128)}), f32[40,8,64,128]{3,2,1,0:T(8,128)}) %all-gather.3.cloned.1.call-update) | async-done | bytes 10485776 | tf_op jit(solution)/shard_map/all_gather | solution.py:272
  377.3 111.4 %shard_map.102 = bf16[20,2,32,64,128]{4,3,2,1,0:T(8,128)(2,1)} custom-call(f32[4,2,5,8,64,128]{5,4,3,2,1,0:T(8,128)} %bitcast.49, bf16[20,2,32,64,128]{4,3,2,1,0:T(8,128)(2,1)} %f_ref.1, bf16[2,128,128]{2,1,0:T(8,128)(2,1)} %pad_maximum_fusion.3.x_ref, bf16[2,128,64]{2,1,0:T(8,128)(2,1)} %pad_maximum_fusion.4.y_ref, bf16[2,256,512]{2,1,0:T(8,128)(2,1)} %constant.69.z_ref, ...), custom_call_target="tpu_custom_call" | custom-call | tf_op jit(solution)/shard_map/pallas_call | solution.py:280
  (45 shorter events, 8.0 us)
Async XLA Ops:
  6.5 231.5 %all-reduce.2.cloned.1.call-start = ((), (), s32[]{:S(2)}) async-start(), calls=%async_computation.1 | async-start | bytes 4194304 | tf_op jit(solution)/shard_map/psum | solution.py:248
  7.3 73.5 %copy-start.2 = (f32[2]{0:T(128)}, f32[2]{0:T(128)S(1)}, u32[]{:S(2)}) copy-start(f32[2]{0:T(128)S(1)} %dynamic-slice_convert_fusion.1.c_ref) | copy-start | bytes 28
  86.4 9.1 %collective-permute-start = (f32[5,32,64,128]{3,2,1,0:T(8,128)}, f32[5,32,64,128]{3,2,1,0:T(8,128)}, u32[]{:S(2)}, u32[]{:S(2)}) collective-permute-start(f32[5,32,64,128]{3,2,1,0:T(8,128)} %dynamic-slice_bitcast_fusion), channel_id=1, source_target_pairs={{0,1},{1,0},{2,3},{3,2},{4,5},{5,4},{6,7},{7,6},{8,9},{9,8},{10,11... | collective-permute-start | bytes 15728648 | tf_op jit(solution)/shard_map/ppermute | solution.py:244
  175.8 201.5 %all-gather.3.cloned.1.call-start = ((), (), s32[]{:S(2)}) async-start(), calls=%async_computation.2 | async-start | bytes 11796480 | tf_op jit(solution)/shard_map/all_gather | solution.py:272
  271.4 3.4 collective-permute-start.1
  273.2 4.6 copy-start
  273.2 5.0 %copy-start.1 = (bf16[20,20]{1,0:T(8,128)(2,1)S(1)}, bf16[20,20]{1,0:T(8,128)(2,1)}, u32[]{:S(2)}) copy-start(bf16[20,20]{1,0:T(8,128)(2,1)} %param.13) | copy-start | bytes 2404
Sparse Core Ops, SparseCore 0:
  175.9 62.0 all-reduce.1
  277.9 99.3 all-gather.2
